TPU v7x, 256 devices: a whole 4x4x8 slice. The times are simulated.
256 devices in a mesh: shot: 8 (over z), trace: 32 (over y, x, core).
Axes of the slice: x: 4, y: 4, z: 8, core: 2. Of those that a mesh axis runs over, the one named last changes fastest.
Arguments:
- gathers: bfloat16 [16, 2048, 4096], P('shot', 'trace'), may hold values from -6 to 6
- first_strided_weight: bfloat16 [4, 128], replicated, may hold values from -3 to 3
- second_strided_weight: bfloat16 [512, 128], replicated, may hold values from -0.25 to 0.25
- second_dilated_weight: bfloat16 [384, 128], replicated, may hold values from -0.3125 to 0.3125
- second_pointwise_weight: bfloat16 [128, 128], replicated, may hold values from -0.5 to 0.5
- third_strided_weight: bfloat16 [512, 128], replicated, may hold values from -0.25 to 0.25
- third_dilated_weight: bfloat16 [384, 128], replicated, may hold values from -0.3125 to 0.3125
- third_pointwise_weight: bfloat16 [128, 128], replicated, may hold values from -0.5 to 0.5
- final_strided_weight: bfloat16 [512, 128], replicated, may hold values from -0.25 to 0.25
- codebooks: bfloat16 [8, 1024, 128], replicated, may hold values from -3 to 3
- codes: int32 [16, 4096, 8, 8], P('shot', 'trace'), may hold values from 0 to 1023
- dest: int32 [8, 32, 256, 1], P('shot', 'trace'), may hold values from 0 to 255; in each aligned block of 256 rows (0 to 255, 256 to 511, ..., all dimensions but the last counted through in order) at most 2 rows name the same one
- bins: int32 [8, 32, 256], P('shot', 'trace'), may hold values from 0 to 63
Outputs:
- stack_code: float32 [16384, 8, 128], P(('shot', 'trace'))
- stack_resid: float32 [16384, 8, 128], P(('shot', 'trace'))
Inputs may be any that keep to these rules, and one draw needn't show every extreme that they name: `dest`: among one device's 256 rows at most 2 name the same owner, a bound that some block reaches of them.
All inputs are finite; a program needn't handle non-finite values.
Results may differ from a plain program's by a relative error of at most 0.0085.
Values may be sent and summed in bfloat16 or wider, within the bound.
A program may use at most 128 MiB of HBM per device.

v0:
```python
import jax
import jax.numpy as jnp
from jax import lax
from jax.experimental import pallas as pl
from jax.experimental.pallas import tpu as pltpu
from jax.sharding import PartitionSpec as P

F32, BF16, I32 = jnp.float32, jnp.bfloat16, jnp.int32
MESH = pl.DeviceIdType.MESH
NZ, NP = 8, 32
ROWS, HALF, FR, C = 256, 128, 8, 128
NB = 8
GROUPS = NP // NB
BINS = 64
SLOTS = 2 * NZ * NP


def elu(x):
    low = jnp.exp(x) - 1.0
    return jnp.maximum(x.astype(BF16), jnp.minimum(low.astype(BF16), 0.0))


def dot(a, b):
    return jnp.dot(a, b, preferred_element_type=F32)


def dot_nt(a, b):
    return lax.dot_general(a, b, (((1,), (1,)), ((), ())), preferred_element_type=F32)


def iota(shape, axis):
    return lax.broadcasted_iota(I32, shape, axis)


def hot(mask):
    return jnp.where(mask, 1.0, 0.0).astype(BF16)


def lanes(parts):
    return jnp.concatenate(parts, axis=1)


def bytes_of(ref, sem):
    return pltpu.make_async_copy(ref, ref, sem)


def residual(skip, act, wd, wp, rows, stack):
    def body(step, carry):
        bases = [6 * (step * stack + n) for n in range(stack)]
        taps = jnp.concatenate(
            [
                lanes(
                    [act[pl.ds(t + 3 * i, 3), rows].reshape(3 * HALF, C) for i in range(4)]
                )
                for t in bases
            ],
            axis=0,
        )
        outer = dot(elu(dot(taps, wd[...])), wp[...])
        for n, t in enumerate(bases):
            for i in range(2):
                piece = outer[n * 3 * HALF : (n + 1) * 3 * HALF, C * i : C * (i + 1)]
                at = pl.ds(t + 3 * i, 3)
                old = skip[at, rows].astype(F32)
                skip[at, rows] = (old + piece.reshape(3, HALF, C)).astype(BF16)
        return carry

    return body


def kernel(
    g, w1_in, w2_in, w2d_in, w2p_in, w3_in, w3d_in, w3p_in, w4_in, cb_in, codes_in, dest, bins,
    out_code, out_latent, out_fold,
    w1, w2, w2d, w2p, w3, w3d, w3p, w4, cb, codes,
    w1_wide, w2d_pair, w2p_pair, w3d_pair, w3p_pair,
    got, s_mid, s_act, t_mid, t_act, order, place, relay, lat,
    meta_tab, meta_z, meta_mid, meta_own, tab, rows_z, rows_mid, rows_own, meta_t, count, dec, x,
    load_sem, own_sem, g_send, g_recv, mz_send, mz_recv, mp_send, mp_recv,
    z_send, z_recv, p_send, p_recv,
):
    z, p = lax.axis_index("shot"), lax.axis_index("trace")

    loads = [
        pltpu.make_async_copy(src, dst, load_sem.at[i])
        for i, (src, dst) in enumerate(
            [
                (codes_in, codes), (w1_in, w1), (w2_in, w2), (w2d_in, w2d), (w2p_in, w2p),
                (w3_in, w3), (w3d_in, w3d), (w3p_in, w3p), (w4_in, w4), (cb_in, cb),
            ]
        )
    ]
    for load in loads:
        load.start()
    own_block = pltpu.make_async_copy(
        g.at[:, :, pl.ds(pl.multiple_of(p * C, C), C)], got.at[p], own_sem
    )
    own_block.start()

    barrier = pltpu.get_barrier_semaphore()

    def greet_plane(j, carry):
        pl.semaphore_signal(
            barrier, inc=1, device_id={"trace": lax.rem(p + j, NP)}, device_id_type=MESH
        )
        return carry

    def greet_z(j, carry):
        pl.semaphore_signal(
            barrier, inc=1, device_id={"shot": lax.rem(z + j, NZ)}, device_id_type=MESH
        )
        return carry

    lax.fori_loop(1, NP, greet_plane, 0)
    lax.fori_loop(1, NZ, greet_z, 0)
    pl.semaphore_wait(barrier, NP - 1 + NZ - 1)

    def send_block(j, carry):
        to = lax.rem(p - j + NP, NP)
        pltpu.make_async_remote_copy(
            src_ref=g.at[:, :, pl.ds(pl.multiple_of(to * C, C), C)],
            dst_ref=got.at[p],
            send_sem=g_send,
            recv_sem=g_recv.at[j // NB],
            device_id={"trace": to},
            device_id_type=MESH,
        ).start()
        return carry

    lax.fori_loop(1, NP, send_block, 0)

    sub, lane = iota((ROWS, ROWS), 0), iota((ROWS, ROWS), 1)
    dest_row = dest[...]
    dest_f = dest_row.astype(F32)
    dest_col = jnp.sum(jnp.where(sub == lane, dest_f, 0.0), axis=1, keepdims=True)
    same = dest_col == dest_f
    rank_row = jnp.sum(jnp.where(same & (sub < lane), 1.0, 0.0), axis=0, keepdims=True)
    rank_col = jnp.sum(jnp.where(same & (lane < sub), 1.0, 0.0), axis=1, keepdims=True)
    seconds_before = jnp.sum(
        jnp.where((rank_col > 0.5) & (sub < lane), 1.0, 0.0), axis=0, keepdims=True
    )
    seconds = jnp.sum(rank_row, axis=1, keepdims=True)
    index = iota((1, ROWS), 1).astype(F32)
    position = jnp.where(rank_row > 0.5, seconds_before, seconds + index - seconds_before)
    order[...] = hot(position == sub.astype(F32))
    owner_hit = dest_row == sub
    slot_hot = [hot(owner_hit & (rank_row < 0.5)), hot(owner_hit & (rank_row > 0.5))]
    for r in range(2):
        place[r] = dot_nt(slot_hot[r], order[...]).astype(BF16)
    i, j = iota((SLOTS, SLOTS), 0), iota((SLOTS, SLOTS), 1)
    relay[...] = hot(j == (i % 16) * 32 + i // 16)

    loads[0].wait()
    ids = lanes([codes[s].reshape(64, HALF) for s in range(2)])
    low, high = ids & 255, ids >> 8
    marks = jnp.where(iota((C, ROWS), 0) == 0, bins[...] + 1, 0)
    meta = jnp.concatenate(
        [part.astype(F32).astype(BF16) for part in (low, high, marks)], axis=0
    )
    for r in range(2):
        meta_tab[:, r] = dot_nt(slot_hot[r], meta).astype(BF16).reshape(NZ, NP, 2 * C)
    meta_z[z] = meta_tab[z]

    def send_meta_z(j, carry):
        to = lax.rem(z + j, NZ)
        pltpu.make_async_remote_copy(
            src_ref=meta_tab.at[to],
            dst_ref=meta_z.at[z],
            send_sem=mz_send,
            recv_sem=mz_recv,
            device_id={"shot": to},
            device_id_type=MESH,
        ).start()
        return carry

    lax.fori_loop(1, NZ, send_meta_z, 0)

    for load in loads[1:9]:
        load.wait()
    tall = jnp.concatenate([w1[...].astype(F32)] * 32, axis=0)
    for t in range(16):
        w1_wide[:, C * t : C * (t + 1)] = jnp.where(iota((C, C), 0) % 64 // 4 == t, tall, 0.0).astype(
            BF16
        )
    zero = jnp.zeros((C, C), BF16)
    for wd, wp, wd_pair, wp_pair in ((w2d, w2p, w2d_pair, w2p_pair), (w3d, w3p, w3d_pair, w3p_pair)):
        wd_pair[0 : 3 * C, 0:C] = wd[...]
        wd_pair[3 * C : 4 * C, 0:C] = zero
        wd_pair[0:C, C : 2 * C] = zero
        wd_pair[C : 4 * C, C : 2 * C] = wd[...]
        wp_pair[0:C, 0:C] = wp[...]
        wp_pair[0:C, C : 2 * C] = zero
        wp_pair[C : 2 * C, 0:C] = zero
        wp_pair[C : 2 * C, C : 2 * C] = wp[...]
    edge = jnp.zeros((ROWS, C), BF16)
    for act, frames in ((s_act, 128), (t_act, 32)):
        for n in range(3):
            act[n] = edge
        for n in range(act.shape[0] - frames - 3):
            act[frames + 3 + n] = edge
    for mid, frames in ((s_mid, 128), (t_mid, 32)):
        for n in range(mid.shape[0] - frames):
            mid[frames + n] = edge

    own_block.wait()
    bytes_of(got.at[pl.ds(0, NB - 1)], g_recv.at[0]).wait()

    def send_meta_p(j, carry):
        to = lax.rem(p + j, NP)
        pltpu.make_async_remote_copy(
            src_ref=meta_mid.at[to],
            dst_ref=meta_own.at[p],
            send_sem=mp_send,
            recv_sem=mp_recv,
            device_id={"trace": to},
            device_id_type=MESH,
        ).start()
        return carry

    def encode_group(i, carry):
        @pl.when(i > 0)
        def _():
            bytes_of(got.at[pl.ds(0, NB)], g_recv.at[i]).wait()

        @pl.when(i == 2)
        def _():
            bytes_of(meta_z.at[pl.ds(0, NZ - 1)], mz_recv).wait()
            moved = dot(relay[...], meta_z[...].reshape(SLOTS, 2 * C)).astype(BF16)
            meta_mid[...] = moved.reshape(NP, 16, 2 * C)
            meta_own[p] = meta_mid[p]
            lax.fori_loop(1, NP, send_meta_p, 0)

        sources = [lax.rem(p + i * NB + n, NP) for n in range(NB)]
        samples = jnp.concatenate([lanes([got[s, 0], got[s, 1]]) for s in sources], axis=0)
        sorted_rows = dot_nt(order[...], samples).astype(BF16)
        for n in range(NB):
            pair = sorted_rows[:, C * (n // 2) : C * (n // 2 + 1)]
            mine = iota((ROWS, C), 1) // 64 == n % 2
            x[n * ROWS : (n + 1) * ROWS] = jnp.where(mine, pair, jnp.zeros_like(pair))

        def quarter(q, carry):
            at = pl.ds(pl.multiple_of(4 * C * q, 4 * C), 4 * C)
            first = elu(dot(x[...], w1_wide[:, at]))
            second = elu(dot(first, w2[...]))
            active = elu(second.astype(F32))
            for n, s in enumerate(sources):
                part = slice(n * ROWS, (n + 1) * ROWS)
                s_mid[4 * s + q] = second[part]
                s_act[4 * s + q + 3] = active[part]
            return carry

        lax.fori_loop(0, 4, quarter, 0)
        return carry

    lax.fori_loop(0, GROUPS, encode_group, 0)

    def send_z(r, c):
        def go(j, carry):
            to = lax.rem(z + j, NZ)
            pltpu.make_async_remote_copy(
                src_ref=tab.at[r, to, pl.ds(2 * c, 2)],
                dst_ref=rows_z.at[z, r, pl.ds(2 * c, 2)],
                send_sem=z_send.at[c],
                recv_sem=z_recv.at[c],
                device_id={"shot": to},
                device_id_type=MESH,
            ).start()
            return carry

        lax.fori_loop(1, NZ, go, 0)

    lat[...] = jnp.zeros_like(lat)

    def encode_half(h, carry):
        rows = pl.ds(pl.multiple_of(h * HALF, HALF), HALF)
        lax.fori_loop(0, 2, residual(s_mid, s_act, w2d_pair, w2p_pair, rows, 11), 0)

        def third(j, carry):
            taps = jnp.concatenate(
                [
                    lanes([s_mid[4 * (16 * j + n) + i, rows] for i in range(4)])
                    for n in range(16)
                ],
                axis=0,
            )
            u = elu(dot(taps, w3[...]))
            active = elu(u.astype(F32))
            t_mid[pl.ds(16 * j, 16), rows] = u.reshape(16, HALF, C)
            t_act[pl.ds(16 * j + 3, 16), rows] = active.reshape(16, HALF, C)
            return carry

        lax.fori_loop(0, 2, third, 0)
        residual(t_mid, t_act, w3d_pair, w3p_pair, rows, 6)(0, 0)
        taps = jnp.concatenate(
            [lanes([t_mid[4 * n + i, rows] for i in range(4)]) for n in range(8)], axis=0
        )
        lat[:, rows] = dot(taps, w4[...]).astype(BF16).reshape(FR, HALF, C)

        r = 1 - h

        def ship(c, carry):
            wide = lanes([lat[2 * c], lat[2 * c + 1]])
            table = dot(place[r], wide).astype(BF16)
            for n in range(2):
                tab[r, :, 2 * c + n] = table[:, C * n : C * (n + 1)].reshape(NZ, NP, C)
            rows_z[z, r, pl.ds(2 * c, 2)] = tab[r, z, pl.ds(2 * c, 2)]
            send_z(r, c)
            return carry

        lax.fori_loop(0, 4, ship, 0)
        return carry

    lax.fori_loop(0, 2, encode_half, 0)

    bytes_of(meta_own.at[pl.ds(0, NP - 1)], mp_recv).wait()
    loads[9].wait()

    meta_t[...] = dot_nt(
        hot(iota((2 * C, 2 * C), 0) == iota((2 * C, 2 * C), 1)),
        meta_own[...].reshape(SLOTS, 2 * C),
    )
    bin_row = meta_t[C : C + 1]
    sub = iota((4 * BINS, SLOTS), 0).astype(F32).astype(BF16)

    def count_codes(f, carry):
        a, b = iota((2 * C, C), 0), iota((2 * C, C), 1)
        picked = dot(meta_own[...].reshape(SLOTS, 2 * C), hot((a == 8 * f + b) & (b < 8))).astype(BF16)
        rows = pl.ds(pl.multiple_of(BINS * f, BINS), BINS)
        wide = iota((SLOTS, 4 * BINS), 1).astype(F32).astype(BF16)
        one, nil = jnp.ones((), BF16), jnp.zeros((), BF16)
        for k in range(8):
            group = meta_t[pl.ds(64 + 8 * f + k, 1)] * BINS + bin_row - 1.0
            low = picked[:, k : k + 1] == wide
            found = dot(
                jnp.where(group.astype(BF16) == sub, one, nil), jnp.where(low, one, nil)
            ).astype(BF16)
            for n in range(4):
                count[k, rows, 256 * n : 256 * (n + 1)] = found[BINS * n : BINS * (n + 1)]
        return carry

    def relay_rows(c, carry):
        lax.fori_loop(2 * c, 2 * c + 2, count_codes, 0)
        bytes_of(rows_z.at[pl.ds(0, NZ - 1), :, pl.ds(2 * c, 2)], z_recv.at[c]).wait()
        both = lanes([rows_z[:, :, 2 * c + n].reshape(SLOTS, C) for n in range(2)])
        moved = dot(relay[...], both).astype(BF16)
        for n in range(2):
            rows_mid[:, 2 * c + n] = moved[:, C * n : C * (n + 1)].reshape(NP, 16, C)
        rows_own[p, pl.ds(2 * c, 2)] = rows_mid[p, pl.ds(2 * c, 2)]

        def send_p(j, carry):
            to = lax.rem(p + j, NP)
            pltpu.make_async_remote_copy(
                src_ref=rows_mid.at[to, pl.ds(2 * c, 2)],
                dst_ref=rows_own.at[p, pl.ds(2 * c, 2)],
                send_sem=p_send.at[c],
                recv_sem=p_recv.at[c],
                device_id={"trace": to},
                device_id_type=MESH,
            ).start()
            return carry

        lax.fori_loop(1, NP, send_p, 0)
        return carry

    lax.fori_loop(0, 4, relay_rows, 0)

    dec[...] = jnp.zeros_like(dec)

    def decode(k, carry):
        dec[...] += dot(count[k], cb[k])
        return carry

    lax.fori_loop(0, 8, decode, 0)
    is_member = bin_row == (iota((BINS, SLOTS), 0) + 1).astype(F32)
    fold = jnp.maximum(jnp.sum(jnp.where(is_member, 1.0, 0.0), axis=1, keepdims=True), 1.0)
    out_fold[...] = jnp.broadcast_to(fold, (BINS, C))
    member = hot(is_member)
    for f in range(FR):
        out_code[:, f, :] = dec[BINS * f : BINS * (f + 1)]
    for c in range(4):
        f0 = 2 * c
        bytes_of(rows_own.at[pl.ds(0, NP - 1), pl.ds(f0, 2)], p_recv.at[c]).wait()
        both = lanes([rows_own[:, f0 + n].reshape(SLOTS, C) for n in range(2)])
        sums = dot(member, both)
        for n in range(2):
            out_latent[:, f0 + n, :] = sums[:, C * n : C * (n + 1)]

    bytes_of(got.at[pl.ds(0, NP - 1)], g_send).wait()
    bytes_of(meta_z.at[pl.ds(0, NZ - 1)], mz_send).wait()
    bytes_of(meta_own.at[pl.ds(0, NP - 1)], mp_send).wait()
    for c in range(4):
        bytes_of(rows_z.at[pl.ds(0, NZ - 1), :, pl.ds(2 * c, 2)], z_send.at[c]).wait()
        bytes_of(rows_own.at[pl.ds(0, NP - 1), pl.ds(2 * c, 2)], p_send.at[c]).wait()


def on_device(
    gathers, w1, w2, w2d, w2p, w3, w3d, w3p, w4, codebooks, codes, dest, bins
):
    hbm, vmem = pl.BlockSpec(memory_space=pl.ANY), pl.BlockSpec(memory_space=pltpu.VMEM)
    scratch = [
        ((4, C), BF16), ((4 * C, C), BF16), ((3 * C, C), BF16), ((C, C), BF16),
        ((4 * C, C), BF16), ((3 * C, C), BF16), ((C, C), BF16), ((4 * C, C), BF16),
        ((8, 1024, C), BF16), ((2, 8, 8, HALF), I32),
        ((C, 16 * C), BF16), ((4 * C, 2 * C), BF16), ((2 * C, 2 * C), BF16),
        ((4 * C, 2 * C), BF16), ((2 * C, 2 * C), BF16),
        ((NP, 2, 64, C), BF16),
        ((132, ROWS, C), BF16), ((138, ROWS, C), BF16),
        ((36, ROWS, C), BF16), ((42, ROWS, C), BF16),
        ((ROWS, ROWS), BF16), ((2, ROWS, ROWS), BF16), ((SLOTS, SLOTS), BF16),
        ((FR, ROWS, C), BF16),
        ((NZ, 2, NP, 2 * C), BF16), ((NZ, 2, NP, 2 * C), BF16),
        ((NP, 16, 2 * C), BF16), ((NP, 16, 2 * C), BF16),
        ((2, NZ, FR, NP, C), BF16), ((NZ, 2, FR, NP, C), BF16),
        ((NP, FR, 16, C), BF16), ((NP, FR, 16, C), BF16),
        ((2 * C, SLOTS), F32), ((8, FR * BINS, 1024), BF16), ((FR * BINS, C), F32),
        ((NB * ROWS, C), BF16),
    ]
    dma = pltpu.SemaphoreType.DMA
    code_sum, latent_sum, fold = pl.pallas_call(
        kernel,
        out_shape=[jax.ShapeDtypeStruct((BINS, FR, C), F32)] * 2
        + [jax.ShapeDtypeStruct((BINS, C), F32)],
        in_specs=[hbm] * 11 + [vmem] * 2,
        out_specs=[vmem] * 3,
        scratch_shapes=[pltpu.VMEM(shape, kind) for shape, kind in scratch]
        + [
            dma((10,)), dma, dma, dma((GROUPS,)), dma, dma, dma, dma,
            dma((4,)), dma((4,)), dma((4,)), dma((4,)),
        ],
        compiler_params=pltpu.CompilerParams(
            collective_id=0, has_side_effects=True, vmem_limit_bytes=60 * 2**20
        ),
        name="codec_stack",
    )(
        gathers, w1, w2, w2d, w2p, w3, w3d, w3p, w4, codebooks,
        codes.transpose(0, 2, 3, 1), dest.reshape(1, ROWS), bins.reshape(1, ROWS),
    )
    fold = fold[:, None, :]
    return code_sum / fold, (latent_sum - code_sum) / fold


def solution(mesh):
    rows4, rows3 = P("shot", "trace", None, None), P("shot", "trace", None)
    out = P(("shot", "trace"), None, None)
    return jax.shard_map(
        on_device,
        mesh=mesh,
        in_specs=(rows3,) + (P(),) * 9 + (rows4, rows4, rows3),
        out_specs=(out, out),
        check_vma=False,
    )
```

profile of v0, /device:TPU:1, one launch (start us, length us, event | category | flops | bytes accessed | tf_op | source)
XLA Modules:
  0.0 87.8 jit_solution(15398178932737353276)
XLA Ops:
  0.6 85.3 %codec_stack.1 = (f32[64,8,128]{2,1,0:T(8,128)}, f32[64,8,128]{2,1,0:T(8,128)}, f32[64,128]{1,0:T(8,128)}) custom-call(bf16[2,64,4096]{2,1,0:T(8,128)(2,1)} %g.1, bf16[4,128]{1,0:T(4,128)(2,1)} %w1_in.1, bf16[512,128]{1,0:T(8,128)(2,1)} %w2_in.1, bf16[384,128]{1,0:T(8,128)(2,1)} %w2d_in.1, bf16[128,128]{1,0:T(8,128)(2,1)} %w2p_in.1, bf16[512,128]{1,0:T(8,128)(2,1)} %w3_in.1, ...), custom_call_target="tpu_custom_call" | custom-call | tf_op jit(solution)/shard_map/codec_stack/pallas_call | solution.py:418
  85.9 1.9 %subtract_divide_fusion = (f32[64,8,128]{2,1,0:T(8,128)}, f32[64,8,128]{2,1,0:T(8,128)}) fusion(f32[64,8,128]{2,1,0:T(8,128)} %get-tuple-element.7, f32[64,8,128]{2,1,0:T(8,128)} %get-tuple-element.5, f32[64,128]{1,0:T(8,128)} %get-tuple-element.6), kind=kLoop, calls=%fused_computation | loop fusion | flops 196608 | bytes 1081344 | tf_op jit(solution)/shard_map/div | solution.py:438
where the time goes:
time: 87.9 us; the launch traced here: 87.8 us
  Pallas kernels  85.3 us (97%)
  other arithmetic  1.87 us (2%)
    pallas_call x1, Pallas kernels, on_device(): pl.pallas_call(kernel, out_shape=[jax.ShapeDtypeStruct((BINS, FR, C), F32...  85.3 us
    div x1, other arithmetic, on_device(): return (code_sum / fold, (latent_sum - code_sum) / fold)  1.87 us

commit v1 on v0

--- a/solution.py
+++ b/solution.py
@@ -11,6 +11,7 @@
 ROWS, HALF, FR, C = 256, 128, 8, 128
 NB = 8
 GROUPS = NP // NB
+STRIDE = 13
 BINS = 64
 SLOTS = 2 * NZ * NP
 
@@ -115,7 +116,7 @@
     pl.semaphore_wait(barrier, NP - 1 + NZ - 1)
 
     def send_block(j, carry):
-        to = lax.rem(p - j + NP, NP)
+        to = lax.rem(p + (NP - STRIDE) * j, NP)
         pltpu.make_async_remote_copy(
             src_ref=g.at[:, :, pl.ds(pl.multiple_of(to * C, C), C)],
             dst_ref=got.at[p],
@@ -161,7 +162,7 @@
     meta_z[z] = meta_tab[z]
 
     def send_meta_z(j, carry):
-        to = lax.rem(z + j, NZ)
+        to = lax.rem(z + 3 * j, NZ)
         pltpu.make_async_remote_copy(
             src_ref=meta_tab.at[to],
             dst_ref=meta_z.at[z],
@@ -205,7 +206,7 @@
     bytes_of(got.at[pl.ds(0, NB - 1)], g_recv.at[0]).wait()
 
     def send_meta_p(j, carry):
-        to = lax.rem(p + j, NP)
+        to = lax.rem(p + STRIDE * j, NP)
         pltpu.make_async_remote_copy(
             src_ref=meta_mid.at[to],
             dst_ref=meta_own.at[p],
@@ -229,7 +230,7 @@
             meta_own[p] = meta_mid[p]
             lax.fori_loop(1, NP, send_meta_p, 0)
 
-        sources = [lax.rem(p + i * NB + n, NP) for n in range(NB)]
+        sources = [lax.rem(p + STRIDE * (i * NB + n), NP) for n in range(NB)]
         samples = jnp.concatenate([lanes([got[s, 0], got[s, 1]]) for s in sources], axis=0)
         sorted_rows = dot_nt(order[...], samples).astype(BF16)
         for n in range(NB):
@@ -255,7 +256,7 @@
 
     def send_z(r, c):
         def go(j, carry):
-            to = lax.rem(z + j, NZ)
+            to = lax.rem(z + 3 * j, NZ)
             pltpu.make_async_remote_copy(
                 src_ref=tab.at[r, to, pl.ds(2 * c, 2)],
                 dst_ref=rows_z.at[z, r, pl.ds(2 * c, 2)],
@@ -347,7 +348,7 @@
         rows_own[p, pl.ds(2 * c, 2)] = rows_mid[p, pl.ds(2 * c, 2)]
 
         def send_p(j, carry):
-            to = lax.rem(p + j, NP)
+            to = lax.rem(p + STRIDE * j, NP)
             pltpu.make_async_remote_copy(
                 src_ref=rows_mid.at[to, pl.ds(2 * c, 2)],
                 dst_ref=rows_own.at[p, pl.ds(2 * c, 2)],

time: 87.9 us -> 86.4 us (0.983)
  Pallas kernels: 85.3 us -> 83.8 us
    pallas_call x1, Pallas kernels: 85.3 us -> 83.8 us  [on_device(): pl.pallas_call(kernel, out_shape=[jax.ShapeDtypeStruct((BINS, FR, C), F32...]
where the time goes in v1:
time: 86.4 us; the launch traced here: 86.3 us
  Pallas kernels  83.8 us (97%)
  other arithmetic  1.87 us (2%)
    pallas_call x1, Pallas kernels, on_device(): pl.pallas_call(kernel, out_shape=[jax.ShapeDtypeStruct((BINS, FR, C), F32...  83.8 us
    div x1, other arithmetic, on_device(): return (code_sum / fold, (latent_sum - code_sum) / fold)  1.87 us

profile of v1, /device:TPU:1, one launch (start us, length us, event | category | flops | bytes accessed | tf_op | source)
XLA Modules:
  0.0 86.3 jit_solution(1983539275793126224)
XLA Ops:
  0.6 83.8 %codec_stack.1 = (f32[64,8,128]{2,1,0:T(8,128)}, f32[64,8,128]{2,1,0:T(8,128)}, f32[64,128]{1,0:T(8,128)}) custom-call(bf16[2,64,4096]{2,1,0:T(8,128)(2,1)} %g.1, bf16[4,128]{1,0:T(4,128)(2,1)} %w1_in.1, bf16[512,128]{1,0:T(8,128)(2,1)} %w2_in.1, bf16[384,128]{1,0:T(8,128)(2,1)} %w2d_in.1, bf16[128,128]{1,0:T(8,128)(2,1)} %w2p_in.1, bf16[512,128]{1,0:T(8,128)(2,1)} %w3_in.1, ...), custom_call_target="tpu_custom_call" | custom-call | tf_op jit(solution)/shard_map/codec_stack/pallas_call | solution.py:419
  84.4 1.9 %subtract_divide_fusion = (f32[64,8,128]{2,1,0:T(8,128)}, f32[64,8,128]{2,1,0:T(8,128)}) fusion(f32[64,8,128]{2,1,0:T(8,128)} %get-tuple-element.7, f32[64,8,128]{2,1,0:T(8,128)} %get-tuple-element.5, f32[64,128]{1,0:T(8,128)} %get-tuple-element.6), kind=kLoop, calls=%fused_computation | loop fusion | flops 196608 | bytes 1081344 | tf_op jit(solution)/shard_map/div | solution.py:439

commit v2 on v1

--- a/solution.py
+++ b/solution.py
@@ -8,7 +8,7 @@
 F32, BF16, I32 = jnp.float32, jnp.bfloat16, jnp.int32
 MESH = pl.DeviceIdType.MESH
 NZ, NP = 8, 32
-ROWS, HALF, FR, C = 256, 128, 8, 128
+ROWS, PART, FR, C = 256, 64, 8, 128
 NB = 8
 GROUPS = NP // NB
 STRIDE = 13
@@ -51,7 +51,7 @@
         taps = jnp.concatenate(
             [
                 lanes(
-                    [act[pl.ds(t + 3 * i, 3), rows].reshape(3 * HALF, C) for i in range(4)]
+                    [act[pl.ds(t + 3 * i, 3), rows].reshape(3 * PART, C) for i in range(4)]
                 )
                 for t in bases
             ],
@@ -60,10 +60,10 @@
         outer = dot(elu(dot(taps, wd[...])), wp[...])
         for n, t in enumerate(bases):
             for i in range(2):
-                piece = outer[n * 3 * HALF : (n + 1) * 3 * HALF, C * i : C * (i + 1)]
+                piece = outer[n * 3 * PART : (n + 1) * 3 * PART, C * i : C * (i + 1)]
                 at = pl.ds(t + 3 * i, 3)
                 old = skip[at, rows].astype(F32)
-                skip[at, rows] = (old + piece.reshape(3, HALF, C)).astype(BF16)
+                skip[at, rows] = (old + piece.reshape(3, PART, C)).astype(BF16)
         return carry
 
     return body
@@ -140,8 +140,12 @@
         jnp.where((rank_col > 0.5) & (sub < lane), 1.0, 0.0), axis=0, keepdims=True
     )
     seconds = jnp.sum(rank_row, axis=1, keepdims=True)
-    index = iota((1, ROWS), 1).astype(F32)
-    position = jnp.where(rank_row > 0.5, seconds_before, seconds + index - seconds_before)
+    away = ((dest_row + (ROWS - NP * lax.rem(z + 4, NZ))) & (ROWS - 1)).astype(F32)
+    away_col = jnp.sum(jnp.where(sub == lane, away, 0.0), axis=1, keepdims=True)
+    firsts_before = jnp.sum(
+        jnp.where((rank_col < 0.5) & (away_col < away), 1.0, 0.0), axis=0, keepdims=True
+    )
+    position = jnp.where(rank_row > 0.5, seconds_before, seconds + firsts_before)
     order[...] = hot(position == sub.astype(F32))
     owner_hit = dest_row == sub
     slot_hot = [hot(owner_hit & (rank_row < 0.5)), hot(owner_hit & (rank_row > 0.5))]
@@ -151,7 +155,7 @@
     relay[...] = hot(j == (i % 16) * 32 + i // 16)
 
     loads[0].wait()
-    ids = lanes([codes[s].reshape(64, HALF) for s in range(2)])
+    ids = lanes([codes[s].reshape(64, C) for s in range(2)])
     low, high = ids & 255, ids >> 8
     marks = jnp.where(iota((C, ROWS), 0) == 0, bins[...] + 1, 0)
     meta = jnp.concatenate(
@@ -254,63 +258,65 @@
 
     lax.fori_loop(0, GROUPS, encode_group, 0)
 
-    def send_z(r, c):
-        def go(j, carry):
-            to = lax.rem(z + 3 * j, NZ)
+    def send_z(r, slot, c, offsets):
+        for offset in offsets:
+            to = lax.rem(z + offset, NZ)
             pltpu.make_async_remote_copy(
-                src_ref=tab.at[r, to, pl.ds(2 * c, 2)],
+                src_ref=tab.at[slot, to, pl.ds(2 * c, 2)],
                 dst_ref=rows_z.at[z, r, pl.ds(2 * c, 2)],
                 send_sem=z_send.at[c],
                 recv_sem=z_recv.at[c],
                 device_id={"shot": to},
                 device_id_type=MESH,
             ).start()
-            return carry
-
-        lax.fori_loop(1, NZ, go, 0)
 
     lat[...] = jnp.zeros_like(lat)
 
-    def encode_half(h, carry):
-        rows = pl.ds(pl.multiple_of(h * HALF, HALF), HALF)
-        lax.fori_loop(0, 2, residual(s_mid, s_act, w2d_pair, w2p_pair, rows, 11), 0)
+    def encode_part(h, carry):
+        rows = pl.ds(pl.multiple_of(h * PART, PART), PART)
+        lax.fori_loop(0, 1, residual(s_mid, s_act, w2d_pair, w2p_pair, rows, 22), 0)
 
         def third(j, carry):
             taps = jnp.concatenate(
                 [
-                    lanes([s_mid[4 * (16 * j + n) + i, rows] for i in range(4)])
-                    for n in range(16)
+                    lanes([s_mid[4 * (32 * j + n) + i, rows] for i in range(4)])
+                    for n in range(32)
                 ],
                 axis=0,
             )
             u = elu(dot(taps, w3[...]))
             active = elu(u.astype(F32))
-            t_mid[pl.ds(16 * j, 16), rows] = u.reshape(16, HALF, C)
-            t_act[pl.ds(16 * j + 3, 16), rows] = active.reshape(16, HALF, C)
+            t_mid[pl.ds(32 * j, 32), rows] = u.reshape(32, PART, C)
+            t_act[pl.ds(32 * j + 3, 32), rows] = active.reshape(32, PART, C)
             return carry
 
-        lax.fori_loop(0, 2, third, 0)
+        third(0, 0)
         residual(t_mid, t_act, w3d_pair, w3p_pair, rows, 6)(0, 0)
         taps = jnp.concatenate(
             [lanes([t_mid[4 * n + i, rows] for i in range(4)]) for n in range(8)], axis=0
         )
-        lat[:, rows] = dot(taps, w4[...]).astype(BF16).reshape(FR, HALF, C)
-
-        r = 1 - h
-
-        def ship(c, carry):
-            wide = lanes([lat[2 * c], lat[2 * c + 1]])
-            table = dot(place[r], wide).astype(BF16)
-            for n in range(2):
-                tab[r, :, 2 * c + n] = table[:, C * n : C * (n + 1)].reshape(NZ, NP, C)
-            rows_z[z, r, pl.ds(2 * c, 2)] = tab[r, z, pl.ds(2 * c, 2)]
-            send_z(r, c)
-            return carry
-
-        lax.fori_loop(0, 4, ship, 0)
-        return carry
-
-    lax.fori_loop(0, 2, encode_half, 0)
+        lat[:, rows] = dot(taps, w4[...]).astype(BF16).reshape(FR, PART, C)
+
+        for part, r, slot, offsets in (
+            (1, 1, 1, (4, 3, 5, 2, 6, 1, 7)), (2, 0, 2, (4, 5)), (3, 0, 0, (3, 6, 2, 7, 1))
+        ):
+
+            @pl.when(h == part)
+            def _(r=r, slot=slot, offsets=offsets):
+                def ship(c, carry):
+                    wide = lanes([lat[2 * c], lat[2 * c + 1]])
+                    table = dot(place[r], wide).astype(BF16)
+                    for n in range(2):
+                        tab[slot, :, 2 * c + n] = table[:, C * n : C * (n + 1)].reshape(NZ, NP, C)
+                    rows_z[z, r, pl.ds(2 * c, 2)] = tab[slot, z, pl.ds(2 * c, 2)]
+                    send_z(r, slot, c, offsets)
+                    return carry
+
+                lax.fori_loop(0, 4, ship, 0)
+
+        return carry
+
+    lax.fori_loop(0, 4, encode_part, 0)
 
     bytes_of(meta_own.at[pl.ds(0, NP - 1)], mp_recv).wait()
     loads[9].wait()
@@ -400,7 +406,7 @@
     scratch = [
         ((4, C), BF16), ((4 * C, C), BF16), ((3 * C, C), BF16), ((C, C), BF16),
         ((4 * C, C), BF16), ((3 * C, C), BF16), ((C, C), BF16), ((4 * C, C), BF16),
-        ((8, 1024, C), BF16), ((2, 8, 8, HALF), I32),
+        ((8, 1024, C), BF16), ((2, 8, 8, C), I32),
         ((C, 16 * C), BF16), ((4 * C, 2 * C), BF16), ((2 * C, 2 * C), BF16),
         ((4 * C, 2 * C), BF16), ((2 * C, 2 * C), BF16),
         ((NP, 2, 64, C), BF16),
@@ -410,7 +416,7 @@
         ((FR, ROWS, C), BF16),
         ((NZ, 2, NP, 2 * C), BF16), ((NZ, 2, NP, 2 * C), BF16),
         ((NP, 16, 2 * C), BF16), ((NP, 16, 2 * C), BF16),
-        ((2, NZ, FR, NP, C), BF16), ((NZ, 2, FR, NP, C), BF16),
+        ((3, NZ, FR, NP, C), BF16), ((NZ, 2, FR, NP, C), BF16),
         ((NP, FR, 16, C), BF16), ((NP, FR, 16, C), BF16),
         ((2 * C, SLOTS), F32), ((8, FR * BINS, 1024), BF16), ((FR * BINS, C), F32),
         ((NB * ROWS, C), BF16),

time: 86.4 us -> 91.8 us (1.062)
  Pallas kernels: 83.8 us -> 89.2 us
    pallas_call x1, Pallas kernels: 83.8 us -> 89.2 us  [on_device(): pl.pallas_call(kernel, out_shape=[jax.ShapeDtypeStruct((BINS, FR, C), F32...]
where the time goes in v2:
time: 91.8 us; the launch traced here: 91.7 us
  Pallas kernels  89.2 us (97%)
  other arithmetic  1.87 us (2%)
    pallas_call x1, Pallas kernels, on_device(): pl.pallas_call(kernel, out_shape=[jax.ShapeDtypeStruct((BINS, FR, C), F32...  89.2 us
    div x1, other arithmetic, on_device(): return (code_sum / fold, (latent_sum - code_sum) / fold)  1.87 us

profile of v2, /device:TPU:1, one launch (start us, length us, event | category | flops | bytes accessed | tf_op | source)
XLA Modules:
  0.0 91.7 jit_solution(4540459501449701854)
XLA Ops:
  0.6 89.2 %codec_stack.1 = (f32[64,8,128]{2,1,0:T(8,128)}, f32[64,8,128]{2,1,0:T(8,128)}, f32[64,128]{1,0:T(8,128)}) custom-call(bf16[2,64,4096]{2,1,0:T(8,128)(2,1)} %g.1, bf16[4,128]{1,0:T(4,128)(2,1)} %w1_in.1, bf16[512,128]{1,0:T(8,128)(2,1)} %w2_in.1, bf16[384,128]{1,0:T(8,128)(2,1)} %w2d_in.1, bf16[128,128]{1,0:T(8,128)(2,1)} %w2p_in.1, bf16[512,128]{1,0:T(8,128)(2,1)} %w3_in.1, ...), custom_call_target="tpu_custom_call" | custom-call | tf_op jit(solution)/shard_map/codec_stack/pallas_call | solution.py:425
  89.8 1.9 %subtract_divide_fusion = (f32[64,8,128]{2,1,0:T(8,128)}, f32[64,8,128]{2,1,0:T(8,128)}) fusion(f32[64,8,128]{2,1,0:T(8,128)} %get-tuple-element.7, f32[64,8,128]{2,1,0:T(8,128)} %get-tuple-element.5, f32[64,128]{1,0:T(8,128)} %get-tuple-element.6), kind=kLoop, calls=%fused_computation | loop fusion | flops 196608 | bytes 1081344 | tf_op jit(solution)/shard_map/div | solution.py:445
